TPU v7x, 512 devices: a whole 4x8x8 slice. The times are simulated.
512 devices in a mesh: expert: 64 (over x, z, core), tensor: 8 (over y).
Axes of the slice: x: 4, y: 8, z: 8, core: 2. Of those that a mesh axis runs over, the one named last changes fastest.
Arguments:
- tokens: bfloat16 [8192, 2048], P('expert', 'tensor'), may hold values from -6 to 6
- cotangent: bfloat16 [8192, 2048], P('expert', 'tensor'), may hold values from -6 to 6
- route_ids: int32 [8192, 6], P('expert'), may hold values from 0 to 63, all different within a row
- route_weights: float32 [8192, 6], P('expert'), may hold values from 0.05 to 0.5
- shared_gate: bfloat16 [1408, 2048], P('tensor'), may hold values from -0.125 to 0.125
- shared_up: bfloat16 [1408, 2048], P('tensor'), may hold values from -0.125 to 0.125
- shared_down: bfloat16 [1408, 2048], P('tensor'), may hold values from -0.15625 to 0.15625
- expert_gate: bfloat16 [64, 1408, 2048], P('expert', 'tensor'), may hold values from -0.125 to 0.125
- expert_up: bfloat16 [64, 1408, 2048], P('expert', 'tensor'), may hold values from -0.125 to 0.125
- expert_down: bfloat16 [64, 1408, 2048], P('expert', 'tensor'), may hold values from -0.15625 to 0.15625
Outputs:
- layer_output: bfloat16 [8192, 2048], P('expert', 'tensor')
- input_grad: bfloat16 [8192, 2048], P('expert', 'tensor')
Inputs may be any that keep to these rules, and one draw needn't show every extreme that they name: `route_ids`: each row names 6 different experts.
All inputs are finite; a program needn't handle non-finite values.
Results may differ from a plain program's by a relative error of at most 0.0051.
Values may be sent and summed in bfloat16 or wider, within the bound.
A program may use at most 64 MiB of HBM per device.

v0:
```python
import jax
import jax.numpy as jnp
from jax import lax
from jax.sharding import PartitionSpec as P


def silu_parts(pre_act):
    sigmoid_value = jax.nn.sigmoid(pre_act)
    return (pre_act * sigmoid_value, sigmoid_value * (1.0 + pre_act * (1.0 - sigmoid_value)))


def on_device(
    tokens,
    cotangent,
    route_ids,
    route_weights,
    shared_gate,
    shared_up,
    shared_down,
    expert_gate,
    expert_up,
    expert_down,
):
    expert_count = lax.axis_size("expert")
    tok_rows, top_count = route_ids.shape
    local_experts = expert_gate.shape[0]
    all_experts = local_experts * expert_count
    capacity = tok_rows * top_count // (2 * all_experts)
    slot_total = all_experts * capacity
    flat_ids = route_ids.reshape(-1)
    one_hot = (flat_ids[:, None] == jnp.arange(all_experts, dtype=jnp.int32)[None, :]).astype(
        jnp.int32
    )
    rank_in = jnp.sum((jnp.cumsum(one_hot, axis=0) - one_hot) * one_hot, axis=1)
    kept_mask = rank_in < capacity
    slot_index = jnp.where(kept_mask, flat_ids * capacity + rank_in, slot_total)
    slot_match = jnp.arange(slot_total, dtype=jnp.int32)[:, None] == slot_index[None, :]
    dispatch = jnp.any(slot_match.reshape(slot_total, tok_rows, top_count), axis=2).astype(
        jnp.bfloat16
    )
    gate_flat = route_weights.reshape(-1)
    slot_gate = jnp.sum(jnp.where(slot_match, gate_flat[None, :], 0.0), axis=1)
    gate_dispatch = dispatch.astype(jnp.float32) * slot_gate[:, None]
    x_full, c_full = (
        lax.all_gather(tokens, "tensor", axis=1, tiled=True),
        lax.all_gather(cotangent, "tensor", axis=1, tiled=True),
    )
    x_slots = jnp.dot(dispatch, x_full, preferred_element_type=jnp.float32).astype(jnp.bfloat16)
    g_slots = (
        slot_gate[:, None] * jnp.dot(dispatch, c_full, preferred_element_type=jnp.float32)
    ).astype(jnp.bfloat16)
    x_recv, g_recv = (
        lax.all_to_all(x_slots, "expert", split_axis=0, concat_axis=0, tiled=True),
        lax.all_to_all(g_slots, "expert", split_axis=0, concat_axis=0, tiled=True),
    )

    def owner_layout(values):
        shaped = values.reshape(expert_count, local_experts, capacity, values.shape[-1])
        return shaped.transpose(1, 0, 2, 3).reshape(
            local_experts, expert_count * capacity, values.shape[-1]
        )

    def source_layout(values):
        shaped = values.reshape(local_experts, expert_count, capacity, values.shape[-1])
        return shaped.transpose(1, 0, 2, 3).reshape(slot_total, values.shape[-1])

    x_own = owner_layout(x_recv)
    g_own = owner_layout(g_recv)
    gate_pre = jnp.einsum("erd,efd->erf", x_own, expert_gate, preferred_element_type=jnp.float32)
    up_pre = jnp.einsum("erd,efd->erf", x_own, expert_up, preferred_element_type=jnp.float32)
    act_value, act_slope = silu_parts(gate_pre)
    hidden = (act_value * up_pre).astype(jnp.bfloat16)
    grad_hidden = jnp.einsum("erd,efd->erf", g_own, expert_down, preferred_element_type=jnp.float32)
    grad_gate = (grad_hidden * up_pre * act_slope).astype(jnp.bfloat16)
    grad_up = (grad_hidden * act_value).astype(jnp.bfloat16)
    value_part = source_layout(
        jnp.einsum("erf,efd->erd", hidden, expert_down, preferred_element_type=jnp.float32).astype(
            jnp.bfloat16
        )
    )
    grads_joined = jnp.concatenate((grad_gate, grad_up), axis=2)
    weights_joined = jnp.concatenate((expert_gate, expert_up), axis=1)
    input_term = jnp.einsum(
        "erf,efd->erd", grads_joined, weights_joined, preferred_element_type=jnp.float32
    )
    input_part = source_layout(input_term.astype(jnp.bfloat16))
    shared_gate_pre = jnp.einsum(
        "td,fd->tf", x_full, shared_gate, preferred_element_type=jnp.float32
    )
    shared_up_pre = jnp.einsum("td,fd->tf", x_full, shared_up, preferred_element_type=jnp.float32)
    shared_act, shared_slope = silu_parts(shared_gate_pre)
    shared_hidden = (shared_act * shared_up_pre).astype(jnp.bfloat16)
    shared_value = jnp.dot(shared_hidden, shared_down, preferred_element_type=jnp.float32)
    shared_grad_hidden = jnp.einsum(
        "td,fd->tf", c_full, shared_down, preferred_element_type=jnp.float32
    )
    shared_grad_gate = (shared_grad_hidden * shared_up_pre * shared_slope).astype(jnp.bfloat16)
    shared_grad_up = (shared_grad_hidden * shared_act).astype(jnp.bfloat16)
    shared_input = jnp.dot(shared_grad_gate, shared_gate, preferred_element_type=jnp.float32)
    shared_input = shared_input + jnp.dot(
        shared_grad_up, shared_up, preferred_element_type=jnp.float32
    )
    value_back, input_back = (
        lax.all_to_all(value_part, "expert", split_axis=0, concat_axis=0, tiled=True),
        lax.all_to_all(input_part, "expert", split_axis=0, concat_axis=0, tiled=True),
    )
    early_value = shared_value + jnp.einsum(
        "st,sd->td",
        gate_dispatch,
        value_back.astype(jnp.float32),
        precision=lax.Precision.HIGHEST,
        preferred_element_type=jnp.float32,
    )
    early_input = shared_input + jnp.einsum(
        "st,sd->td",
        dispatch,
        input_back,
        precision=lax.Precision.HIGHEST,
        preferred_element_type=jnp.float32,
    )
    value_total, input_total = (
        lax.psum_scatter(early_value, "tensor", scatter_dimension=1, tiled=True),
        lax.psum_scatter(early_input, "tensor", scatter_dimension=1, tiled=True),
    )
    return (value_total.astype(jnp.bfloat16), input_total.astype(jnp.bfloat16))


def solution(mesh):
    in_specs = (
        P("expert", "tensor"),
        P("expert", "tensor"),
        P("expert", None),
        P("expert", None),
        P("tensor", None),
        P("tensor", None),
        P("tensor", None),
        P("expert", "tensor", None),
        P("expert", "tensor", None),
        P("expert", "tensor", None),
    )
    out_specs = (P("expert", "tensor"), P("expert", "tensor"))
    return jax.shard_map(
        on_device, mesh=mesh, in_specs=in_specs, out_specs=out_specs, check_vma=False
    )
```

profile of v0, /device:TPU:2, one launch (start us, length us, event | category | flops | bytes accessed | tf_op | source)
XLA Modules:
  0.0 333.4 jit_solution(1822526318146382311)
XLA Ops:
  9.0 27.1 %all_gather.6 = bf16[128,2048]{1,0:T(8,128)(2,1)S(1)} all-gather(bf16[128,256]{1,0:T(8,128)(2,1)} %param.10), channel_id=1, replica_groups=mesh['expert'=64,'tensor'=8] {'tensor'}, dimensions={1}, use_global_device_ids=true | all-gather | bytes 589824 | tf_op jit(solution)/shard_map/all_gather | solution.py:45
  36.3 1.8 reduce-window.6
  39.5 1.6 all_to_all.32
  41.1 14.0 %all-to-all-start = ((bf16[64,6,2048]{2,1,0:T(8,128)(2,1)}), bf16[64,6,2048]{2,1,0:T(8,128)(2,1)S(1)}, u32[]{:S(2)}, u32[]{:S(2)}) async-start(bf16[64,6,2048]{2,1,0:T(8,128)(2,1)} %all_to_all.32), calls=%async_computation | async-start | bytes 4194304 | tf_op jit(solution)/shard_map/all_to_all | solution.py:53
  55.6 25.5 %all_gather.7 = bf16[128,2048]{1,0:T(8,128)(2,1)S(1)} all-gather(bf16[128,256]{1,0:T(8,128)(2,1)S(1)} %copy-done.14), channel_id=1, replica_groups=mesh['expert'=64,'tensor'=8] {'tensor'}, dimensions={1}, use_global_device_ids=true | all-gather | bytes 589824 | tf_op jit(solution)/shard_map/all_gather | solution.py:46
  81.9 1.7 multiply_convert_fusion
  83.6 3.7 %all_to_all.38 = bf16[64,6,2048]{2,1,0:T(8,128)(2,1)} reshape(bf16[384,2048]{1,0:T(8,128)(2,1)} %multiply_convert_fusion) | data formatting | bytes 3145728 | tf_op jit(solution)/shard_map/all_to_all | solution.py:54
  87.3 17.3 %all-to-all-done = bf16[64,6,2048]{2,1,0:T(8,128)(2,1)S(1)} async-done(((bf16[64,6,2048]{2,1,0:T(8,128)(2,1)}), bf16[64,6,2048]{2,1,0:T(8,128)(2,1)S(1)}, u32[]{:S(2)}, u32[]{:S(2)}) %all-to-all-start) | async-done | bytes 1572896 | tf_op jit(solution)/shard_map/all_to_all | solution.py:53
  105.9 7.7 %all-to-all-start.2 = ((bf16[64,6,2048]{2,1,0:T(8,128)(2,1)}), bf16[64,6,2048]{2,1,0:T(8,128)(2,1)}, u32[]{:S(2)}, u32[]{:S(2)}) async-start(bf16[64,6,2048]{2,1,0:T(8,128)(2,1)} %all_to_all.38), calls=%async_computation.3 | async-start | bytes 4194304 | tf_op jit(solution)/shard_map/all_to_all | solution.py:54
  113.6 2.6 all_to_all.34
  116.3 1.8 fusion.6
  121.7 41.4 %all-to-all-done.2 = bf16[64,6,2048]{2,1,0:T(8,128)(2,1)} async-done(((bf16[64,6,2048]{2,1,0:T(8,128)(2,1)}), bf16[64,6,2048]{2,1,0:T(8,128)(2,1)}, u32[]{:S(2)}, u32[]{:S(2)}) %all-to-all-start.2) | async-done | bytes 1572896 | tf_op jit(solution)/shard_map/all_to_all | solution.py:54
  163.1 7.5 %all-to-all-start.1 = ((bf16[64,6,2048]{2,1,0:T(8,128)(2,1)}), bf16[64,6,2048]{2,1,0:T(8,128)(2,1)S(1)}, u32[]{:S(2)}, u32[]{:S(2)}) async-start(bf16[64,6,2048]{2,1,0:T(8,128)(2,1)} %all_to_all.35), calls=%async_computation.1 | async-start | bytes 4194304 | tf_op jit(solution)/shard_map/all_to_all | solution.py:104
  170.6 3.7 %all_to_all.40 = bf16[384,2048]{1,0:T(8,128)(2,1)} reshape(bf16[64,6,2048]{2,1,0:T(8,128)(2,1)} %all-to-all-done.2) | data formatting | bytes 3145728 | tf_op jit(solution)/shard_map/all_to_all | solution.py:54
  174.4 2.3 fusion.20
  176.7 2.2 convolution_convert_fusion.1
  178.9 3.7 %all_to_all.41 = bf16[64,6,2048]{2,1,0:T(8,128)(2,1)} reshape(bf16[384,2048]{1,0:T(8,128)(2,1)} %convolution_convert_fusion.1) | data formatting | bytes 3145728 | tf_op jit(solution)/shard_map/all_to_all | solution.py:105
  182.5 37.6 %all-to-all-done.1 = bf16[64,6,2048]{2,1,0:T(8,128)(2,1)S(1)} async-done(((bf16[64,6,2048]{2,1,0:T(8,128)(2,1)}), bf16[64,6,2048]{2,1,0:T(8,128)(2,1)S(1)}, u32[]{:S(2)}, u32[]{:S(2)}) %all-to-all-start.1) | async-done | bytes 1572896 | tf_op jit(solution)/shard_map/all_to_all | solution.py:104
  221.5 7.5 %all-to-all-start.3 = ((bf16[64,6,2048]{2,1,0:T(8,128)(2,1)}), bf16[64,6,2048]{2,1,0:T(8,128)(2,1)S(1)}, u32[]{:S(2)}, u32[]{:S(2)}) async-start(bf16[64,6,2048]{2,1,0:T(8,128)(2,1)} %all_to_all.41), calls=%async_computation.4 | async-start | bytes 4194304 | tf_op jit(solution)/shard_map/all_to_all | solution.py:105
  233.7 3.7 %all_to_all.37 = bf16[384,2048]{1,0:T(8,128)(2,1)} reshape(bf16[64,6,2048]{2,1,0:T(8,128)(2,1)} %copy-done.1) | data formatting | bytes 3145728 | tf_op jit(solution)/shard_map/all_to_all | solution.py:104
  237.4 3.9 %convolution_add_fusion.2 = f32[128,2048]{1,0:T(8,128)} fusion(f32[128,2048]{1,0:T(8,128)} %fusion.25, bf16[384,2048]{1,0:T(8,128)(2,1)} %all_to_all.37, f32[384]{0:T(512)S(1)} %select_reduce_fusion, pred[384,128]{1,0:T(8,128)(4,1)S(1)} %fusion.2), kind=kOutput, calls=%fused_computation.6 | convolution fusion | flops 1208369152 | bytes 3720704 | tf_op jit(solution)/shard_map/st,sd->td/dot_general | solution.py:107
  245.6 33.0 %all-to-all-done.3 = bf16[64,6,2048]{2,1,0:T(8,128)(2,1)S(1)} async-done(((bf16[64,6,2048]{2,1,0:T(8,128)(2,1)}), bf16[64,6,2048]{2,1,0:T(8,128)(2,1)S(1)}, u32[]{:S(2)}, u32[]{:S(2)}) %all-to-all-start.3) | async-done | bytes 1572896 | tf_op jit(solution)/shard_map/all_to_all | solution.py:105
  280.0 3.2 convolution_add_fusion
  284.8 40.3 %reduce-scatter.5.cloned.1.call-done = f32[128,256]{1,0:T(8,128)} async-done(((f32[128,2048]{1,0:T(8,128)}), f32[128,256]{1,0:T(8,128)}) %reduce-scatter.5.cloned.1.call-update) | async-done | bytes 131088 | tf_op jit(solution)/shard_map/reduce_scatter | solution.py:123
  (67 shorter events, 24.2 us)
Async XLA Ops:
  7.2 112.4 %copy-start = (bf16[1,176,2048]{2,1,0:T(8,128)(2,1)S(1)}, bf16[1,176,2048]{2,1,0:T(8,128)(2,1)}, u32[]{:S(2)}) copy-start(bf16[1,176,2048]{2,1,0:T(8,128)(2,1)} %param.19) | copy-start | bytes 2162692
  41.1 14.0 %copy-start.15 = (f32[128,6]{0,1:T(8,128)S(1)}, f32[128,6]{0,1:T(8,128)}, u32[]{:S(2)}) copy-start(f32[128,6]{0,1:T(8,128)} %param.13) | copy-start | bytes 9220
  41.1 14.5 %copy-start.14 = (bf16[128,256]{1,0:T(8,128)(2,1)S(1)}, bf16[128,256]{1,0:T(8,128)(2,1)}, u32[]{:S(2)}) copy-start(bf16[128,256]{1,0:T(8,128)(2,1)} %param.11) | copy-start | bytes 196612
  41.1 63.5 %all-to-all-start = ((bf16[64,6,2048]{2,1,0:T(8,128)(2,1)}), bf16[64,6,2048]{2,1,0:T(8,128)(2,1)S(1)}, u32[]{:S(2)}, u32[]{:S(2)}) async-start(bf16[64,6,2048]{2,1,0:T(8,128)(2,1)} %all_to_all.32), calls=%async_computation | async-start | bytes 4194304 | tf_op jit(solution)/shard_map/all_to_all | solution.py:53
  81.1 0.8 copy-start.3
  104.6 1.3 copy-start.2
  105.9 57.2 %all-to-all-start.2 = ((bf16[64,6,2048]{2,1,0:T(8,128)(2,1)}), bf16[64,6,2048]{2,1,0:T(8,128)(2,1)}, u32[]{:S(2)}, u32[]{:S(2)}) async-start(bf16[64,6,2048]{2,1,0:T(8,128)(2,1)} %all_to_all.38), calls=%async_computation.3 | async-start | bytes 4194304 | tf_op jit(solution)/shard_map/all_to_all | solution.py:54
  116.3 1.9 copy-start.12
  118.1 2.0 copy-start.8
  118.8 0.7 copy-start.9
  163.1 57.1 %all-to-all-start.1 = ((bf16[64,6,2048]{2,1,0:T(8,128)(2,1)}), bf16[64,6,2048]{2,1,0:T(8,128)(2,1)S(1)}, u32[]{:S(2)}, u32[]{:S(2)}) async-start(bf16[64,6,2048]{2,1,0:T(8,128)(2,1)} %all_to_all.35), calls=%async_computation.1 | async-start | bytes 4194304 | tf_op jit(solution)/shard_map/all_to_all | solution.py:104
  174.4 2.3 copy-start.11
  174.4 2.3 copy-start.13
  220.2 1.3 copy-start.1
  221.5 57.1 %all-to-all-start.3 = ((bf16[64,6,2048]{2,1,0:T(8,128)(2,1)}), bf16[64,6,2048]{2,1,0:T(8,128)(2,1)S(1)}, u32[]{:S(2)}, u32[]{:S(2)}) async-start(bf16[64,6,2048]{2,1,0:T(8,128)(2,1)} %all_to_all.41), calls=%async_computation.4 | async-start | bytes 4194304 | tf_op jit(solution)/shard_map/all_to_all | solution.py:105
  229.0 54.2 %reduce-scatter.3.cloned.1.call-start = ((), (), s32[]{:S(2)}) async-start(), calls=%async_computation.6 | async-start | bytes 1179648 | tf_op jit(solution)/shard_map/reduce_scatter | solution.py:122
  229.2 3.1 copy-start.5
  230.8 1.5 copy-start.10
  237.4 3.9 %copy-start.4 = (bf16[128,2048]{1,0:T(8,128)(2,1)S(1)}, bf16[128,2048]{1,0:T(8,128)(2,1)}, u32[]{:S(2)}) copy-start(bf16[128,2048]{1,0:T(8,128)(2,1)} %copy-done.3) | copy-start | bytes 1572868
  241.3 83.8 %reduce-scatter.5.cloned.1.call-start = ((), (), s32[]{:S(2)}) async-start(), calls=%async_computation.7 | async-start | bytes 1179648 | tf_op jit(solution)/shard_map/reduce_scatter | solution.py:123
  241.4 1.6 copy-start.6
  241.4 2.8 copy-start.7
Sparse Core Ops, SparseCore 0:
  241.4 40.5 reduce-scatter.2
  284.8 40.1 reduce-scatter.4
where the time goes:
time: 335 us; the launch traced here: 333 us
  waiting for transfers between devices  170 us (51%)
  blocking collectives  52.6 us (16%)
  starting transfers between devices  37 us (11%)
  local copies, waits for them, and re-layouts  28.1 us (8%)
  matrix products  25.5 us (8%)
  between operations  14.4 us (4%)
  other arithmetic  6.19 us (2%)
    all_to_all x1, waiting for transfers between devices, on_device(): lax.all_to_all(g_slots, 'expert', split_axis=0, concat_axis=0, tiled=True)  41.4 us
    reduce_scatter x1, waiting for transfers between devices, on_device(): lax.psum_scatter(early_input, 'tensor', scatter_dimension=1, tiled=True)  40.3 us
    all_to_all x1, waiting for transfers between devices, on_device(): lax.all_to_all(value_part, 'expert', split_axis=0, concat_axis=0, tiled=T...  37.6 us
    all_to_all x1, waiting for transfers between devices, on_device(): lax.all_to_all(input_part, 'expert', split_axis=0, concat_axis=0, tiled=T...  33 us
    all_gather x1, blocking collectives, on_device(): lax.all_gather(tokens, 'tensor', axis=1, tiled=True)  27.1 us
    all_gather x1, blocking collectives, on_device(): lax.all_gather(cotangent, 'tensor', axis=1, tiled=True)  25.5 us
    all_to_all x1, waiting for transfers between devices, on_device(): lax.all_to_all(x_slots, 'expert', split_axis=0, concat_axis=0, tiled=True)  17.3 us
    all_to_all x1, starting transfers between devices, on_device(): lax.all_to_all(x_slots, 'expert', split_axis=0, concat_axis=0, tiled=True)  14 us
  transfers between devices with their start and end apart: 6, of which 5 were waited for; matrix products, arithmetic and copies ran while one was open for 8% of the time, Pallas kernels for 0%

commit v1 on v0

--- a/solution.py
+++ b/solution.py
@@ -2,6 +2,13 @@
 import jax.numpy as jnp
 from jax import lax
 from jax.sharding import PartitionSpec as P
+
+
+def all_by_exchange(x, name, along):
+    n_dev = lax.axis_size(name)
+    blocks = jnp.stack([x for _ in range(n_dev)])
+    blocks = lax.all_to_all(blocks, name, split_axis=0, concat_axis=0)
+    return jnp.concatenate(blocks, axis=along)
 
 
 def silu_parts(pre_act):
@@ -43,7 +50,7 @@
     gate_dispatch = dispatch.astype(jnp.float32) * slot_gate[:, None]
     x_full, c_full = (
         lax.all_gather(tokens, "tensor", axis=1, tiled=True),
-        lax.all_gather(cotangent, "tensor", axis=1, tiled=True),
+        all_by_exchange(cotangent, "tensor", 1),
     )
     x_slots = jnp.dot(dispatch, x_full, preferred_element_type=jnp.float32).astype(jnp.bfloat16)
     g_slots = (

time: 335 us -> 347 us (1.036)
  waiting for transfers between devices: 170 us -> 195 us
  blocking collectives: 52.6 us -> 31 us
  starting transfers between devices: 37 us -> 44 us
    all_gather x1 -> x0, blocking collectives: 25.5 us -> none  [on_device(): lax.all_gather(cotangent, 'tensor', axis=1, tiled=True)]
    all_to_all x1, waiting for transfers between devices: 17.3 us -> 42.6 us  [on_device(): lax.all_to_all(x_slots, 'expert', split_axis=0, concat_axis=0, tiled=True)]
    all_to_all x0 -> x1, starting transfers between devices: none -> 7.1 us  [all_by_exchange(): blocks = lax.all_to_all(blocks, name, split_axis=0, concat_axis=0)]
    all_gather x1, blocking collectives: 27.1 us -> 31 us  [on_device(): lax.all_gather(tokens, 'tensor', axis=1, tiled=True)]
  transfers between devices with their start and end apart: 6 -> 7, of which waited for: 5 -> 5; matrix products, arithmetic and copies ran while one was open for 8% -> 9% of each run, Pallas kernels for 0% -> 0%
where the time goes in v1:
time: 347 us; the launch traced here: 346 us
  waiting for transfers between devices  195 us (56%)
  starting transfers between devices  44 us (13%)
  blocking collectives  31 us (9%)
  local copies, waits for them, and re-layouts  29.4 us (8%)
  matrix products  26.5 us (8%)
  between operations  14.4 us (4%)
  other arithmetic  5.44 us (2%)
    all_to_all x1, waiting for transfers between devices, on_device(): lax.all_to_all(x_slots, 'expert', split_axis=0, concat_axis=0, tiled=True)  42.6 us
    all_to_all x1, waiting for transfers between devices, on_device(): lax.all_to_all(g_slots, 'expert', split_axis=0, concat_axis=0, tiled=True)  41.3 us
    reduce_scatter x1, waiting for transfers between devices, on_device(): lax.psum_scatter(early_input, 'tensor', scatter_dimension=1, tiled=True)  40.2 us
    all_to_all x1, waiting for transfers between devices, on_device(): lax.all_to_all(value_part, 'expert', split_axis=0, concat_axis=0, tiled=T...  37.6 us
    all_to_all x1, waiting for transfers between devices, on_device(): lax.all_to_all(input_part, 'expert', split_axis=0, concat_axis=0, tiled=T...  33 us
    all_gather x1, blocking collectives, on_device(): lax.all_gather(tokens, 'tensor', axis=1, tiled=True)  31 us
    all_to_all x1, starting transfers between devices, on_device(): lax.all_to_all(x_slots, 'expert', split_axis=0, concat_axis=0, tiled=True)  13.9 us
    all_to_all x1, starting transfers between devices, on_device(): lax.all_to_all(g_slots, 'expert', split_axis=0, concat_axis=0, tiled=True)  7.71 us
  transfers between devices with their start and end apart: 7, of which 5 were waited for; matrix products, arithmetic and copies ran while one was open for 9% of the time, Pallas kernels for 0%

profile of v1, /device:TPU:2, one launch (start us, length us, event | category | flops | bytes accessed | tf_op | source)
XLA Modules:
  0.0 345.6 jit_solution(14536998617973455682)
XLA Ops:
  9.1 7.1 %all-to-all-start.2 = ((bf16[8,128,256]{1,2,0:T(8,128)(2,1)}), bf16[8,128,256]{1,2,0:T(8,128)(2,1)S(1)}, u32[]{:S(2)}, u32[]{:S(2)}) async-start(bf16[8,128,256]{1,2,0:T(8,128)(2,1)} %stack.2), calls=%async_computation.3 | async-start | bytes 1048576 | tf_op jit(solution)/shard_map/all_to_all | solution.py:10
  16.6 1.8 reduce-window.6
  19.4 31.0 %all_gather.3 = bf16[128,2048]{1,0:T(8,128)(2,1)S(1)} all-gather(bf16[128,256]{1,0:T(8,128)(2,1)S(1)} %copy-done.14), channel_id=1, replica_groups=mesh['expert'=64,'tensor'=8] {'tensor'}, dimensions={1}, use_global_device_ids=true | all-gather | bytes 589824 | tf_op jit(solution)/shard_map/all_gather | solution.py:52
  50.9 1.6 all_to_all.35
  53.4 13.9 %all-to-all-start = ((bf16[64,6,2048]{2,1,0:T(8,128)(2,1)}), bf16[64,6,2048]{2,1,0:T(8,128)(2,1)S(1)}, u32[]{:S(2)}, u32[]{:S(2)}) async-start(bf16[64,6,2048]{2,1,0:T(8,128)(2,1)} %all_to_all.35), calls=%async_computation | async-start | bytes 4194304 | tf_op jit(solution)/shard_map/all_to_all | solution.py:60
  67.7 2.8 multiply_convert_fusion
  70.5 3.7 %all_to_all.42 = bf16[64,6,2048]{2,1,0:T(8,128)(2,1)} reshape(bf16[384,2048]{1,0:T(8,128)(2,1)} %multiply_convert_fusion) | data formatting | bytes 3145728 | tf_op jit(solution)/shard_map/all_to_all | solution.py:61
  74.2 42.6 %all-to-all-done = bf16[64,6,2048]{2,1,0:T(8,128)(2,1)S(1)} async-done(((bf16[64,6,2048]{2,1,0:T(8,128)(2,1)}), bf16[64,6,2048]{2,1,0:T(8,128)(2,1)S(1)}, u32[]{:S(2)}, u32[]{:S(2)}) %all-to-all-start) | async-done | bytes 1572896 | tf_op jit(solution)/shard_map/all_to_all | solution.py:60
  118.1 7.7 %all-to-all-start.3 = ((bf16[64,6,2048]{2,1,0:T(8,128)(2,1)}), bf16[64,6,2048]{2,1,0:T(8,128)(2,1)}, u32[]{:S(2)}, u32[]{:S(2)}) async-start(bf16[64,6,2048]{2,1,0:T(8,128)(2,1)} %all_to_all.42), calls=%async_computation.4 | async-start | bytes 4194304 | tf_op jit(solution)/shard_map/all_to_all | solution.py:61
  125.8 2.6 all_to_all.37
  128.5 1.8 fusion.6
  133.9 41.3 %all-to-all-done.3 = bf16[64,6,2048]{2,1,0:T(8,128)(2,1)} async-done(((bf16[64,6,2048]{2,1,0:T(8,128)(2,1)}), bf16[64,6,2048]{2,1,0:T(8,128)(2,1)}, u32[]{:S(2)}, u32[]{:S(2)}) %all-to-all-start.3) | async-done | bytes 1572896 | tf_op jit(solution)/shard_map/all_to_all | solution.py:61
  175.3 7.5 %all-to-all-start.1 = ((bf16[64,6,2048]{2,1,0:T(8,128)(2,1)}), bf16[64,6,2048]{2,1,0:T(8,128)(2,1)S(1)}, u32[]{:S(2)}, u32[]{:S(2)}) async-start(bf16[64,6,2048]{2,1,0:T(8,128)(2,1)} %all_to_all.38), calls=%async_computation.1 | async-start | bytes 4194304 | tf_op jit(solution)/shard_map/all_to_all | solution.py:111
  182.8 3.8 %all_to_all.44 = bf16[384,2048]{1,0:T(8,128)(2,1)} reshape(bf16[64,6,2048]{2,1,0:T(8,128)(2,1)} %all-to-all-done.3) | data formatting | bytes 3145728 | tf_op jit(solution)/shard_map/all_to_all | solution.py:61
  186.6 2.3 fusion.20
  188.9 2.2 convolution_convert_fusion.1
  191.1 3.7 %all_to_all.45 = bf16[64,6,2048]{2,1,0:T(8,128)(2,1)} reshape(bf16[384,2048]{1,0:T(8,128)(2,1)} %convolution_convert_fusion.1) | data formatting | bytes 3145728 | tf_op jit(solution)/shard_map/all_to_all | solution.py:112
  194.8 37.6 %all-to-all-done.1 = bf16[64,6,2048]{2,1,0:T(8,128)(2,1)S(1)} async-done(((bf16[64,6,2048]{2,1,0:T(8,128)(2,1)}), bf16[64,6,2048]{2,1,0:T(8,128)(2,1)S(1)}, u32[]{:S(2)}, u32[]{:S(2)}) %all-to-all-start.1) | async-done | bytes 1572896 | tf_op jit(solution)/shard_map/all_to_all | solution.py:111
  233.7 7.5 %all-to-all-start.4 = ((bf16[64,6,2048]{2,1,0:T(8,128)(2,1)}), bf16[64,6,2048]{2,1,0:T(8,128)(2,1)S(1)}, u32[]{:S(2)}, u32[]{:S(2)}) async-start(bf16[64,6,2048]{2,1,0:T(8,128)(2,1)} %all_to_all.45), calls=%async_computation.5 | async-start | bytes 4194304 | tf_op jit(solution)/shard_map/all_to_all | solution.py:112
  245.9 3.7 %all_to_all.40 = bf16[384,2048]{1,0:T(8,128)(2,1)} reshape(bf16[64,6,2048]{2,1,0:T(8,128)(2,1)} %copy-done.1) | data formatting | bytes 3145728 | tf_op jit(solution)/shard_map/all_to_all | solution.py:111
  249.6 3.9 %convolution_add_fusion.2 = f32[128,2048]{1,0:T(8,128)} fusion(f32[128,2048]{1,0:T(8,128)} %fusion.25, bf16[384,2048]{1,0:T(8,128)(2,1)} %all_to_all.40, f32[384]{0:T(512)S(1)} %select_reduce_fusion, pred[384,128]{1,0:T(8,128)(4,1)S(1)} %fusion.2), kind=kOutput, calls=%fused_computation.6 | convolution fusion | flops 1208369152 | bytes 3720704 | tf_op jit(solution)/shard_map/st,sd->td/dot_general | solution.py:114
  257.7 33.0 %all-to-all-done.4 = bf16[64,6,2048]{2,1,0:T(8,128)(2,1)S(1)} async-done(((bf16[64,6,2048]{2,1,0:T(8,128)(2,1)}), bf16[64,6,2048]{2,1,0:T(8,128)(2,1)S(1)}, u32[]{:S(2)}, u32[]{:S(2)}) %all-to-all-start.4) | async-done | bytes 1572896 | tf_op jit(solution)/shard_map/all_to_all | solution.py:112
  292.2 3.2 convolution_add_fusion
  297.0 40.2 %reduce-scatter.5.cloned.1.call-done = f32[128,256]{1,0:T(8,128)} async-done(((f32[128,2048]{1,0:T(8,128)}), f32[128,256]{1,0:T(8,128)}) %reduce-scatter.5.cloned.1.call-update) | async-done | bytes 131088 | tf_op jit(solution)/shard_map/reduce_scatter | solution.py:130
  (72 shorter events, 24.7 us)
Async XLA Ops:
  7.2 124.5 %copy-start = (bf16[1,176,2048]{2,1,0:T(8,128)(2,1)S(1)}, bf16[1,176,2048]{2,1,0:T(8,128)(2,1)}, u32[]{:S(2)}) copy-start(bf16[1,176,2048]{2,1,0:T(8,128)(2,1)} %param.19) | copy-start | bytes 2162692
  7.2 9.0 %copy-start.15 = (s32[128,6]{0,1:T(8,128)S(1)}, s32[128,6]{0,1:T(8,128)}, u32[]{:S(2)}) copy-start(s32[128,6]{0,1:T(8,128)} %param.12) | copy-start | bytes 9220
  8.2 11.1 %copy-start.14 = (bf16[128,256]{1,0:T(8,128)(2,1)S(1)}, bf16[128,256]{1,0:T(8,128)(2,1)}, u32[]{:S(2)}) copy-start(bf16[128,256]{1,0:T(8,128)(2,1)} %param.10) | copy-start | bytes 196612
  9.1 43.5 %all-to-all-start.2 = ((bf16[8,128,256]{1,2,0:T(8,128)(2,1)}), bf16[8,128,256]{1,2,0:T(8,128)(2,1)S(1)}, u32[]{:S(2)}, u32[]{:S(2)}) async-start(bf16[8,128,256]{1,2,0:T(8,128)(2,1)} %stack.2), calls=%async_computation.3 | async-start | bytes 1048576 | tf_op jit(solution)/shard_map/all_to_all | solution.py:10
  52.6 14.7 %copy-start.16 = (f32[128,6]{0,1:T(8,128)S(1)}, f32[128,6]{0,1:T(8,128)}, u32[]{:S(2)}) copy-start(f32[128,6]{0,1:T(8,128)} %param.13) | copy-start | bytes 9220
  52.6 0.8 copy-start.3
  53.4 63.4 %all-to-all-start = ((bf16[64,6,2048]{2,1,0:T(8,128)(2,1)}), bf16[64,6,2048]{2,1,0:T(8,128)(2,1)S(1)}, u32[]{:S(2)}, u32[]{:S(2)}) async-start(bf16[64,6,2048]{2,1,0:T(8,128)(2,1)} %all_to_all.35), calls=%async_computation | async-start | bytes 4194304 | tf_op jit(solution)/shard_map/all_to_all | solution.py:60
  116.8 1.3 copy-start.2
  118.1 57.2 %all-to-all-start.3 = ((bf16[64,6,2048]{2,1,0:T(8,128)(2,1)}), bf16[64,6,2048]{2,1,0:T(8,128)(2,1)}, u32[]{:S(2)}, u32[]{:S(2)}) async-start(bf16[64,6,2048]{2,1,0:T(8,128)(2,1)} %all_to_all.42), calls=%async_computation.4 | async-start | bytes 4194304 | tf_op jit(solution)/shard_map/all_to_all | solution.py:61
  128.4 1.9 copy-start.12
  130.3 2.0 copy-start.8
  131.0 0.7 copy-start.9
  175.3 57.1 %all-to-all-start.1 = ((bf16[64,6,2048]{2,1,0:T(8,128)(2,1)}), bf16[64,6,2048]{2,1,0:T(8,128)(2,1)S(1)}, u32[]{:S(2)}, u32[]{:S(2)}) async-start(bf16[64,6,2048]{2,1,0:T(8,128)(2,1)} %all_to_all.38), calls=%async_computation.1 | async-start | bytes 4194304 | tf_op jit(solution)/shard_map/all_to_all | solution.py:111
  186.6 2.3 copy-start.11
  186.6 2.3 copy-start.13
  232.3 1.3 copy-start.1
  233.7 57.1 %all-to-all-start.4 = ((bf16[64,6,2048]{2,1,0:T(8,128)(2,1)}), bf16[64,6,2048]{2,1,0:T(8,128)(2,1)S(1)}, u32[]{:S(2)}, u32[]{:S(2)}) async-start(bf16[64,6,2048]{2,1,0:T(8,128)(2,1)} %all_to_all.45), calls=%async_computation.5 | async-start | bytes 4194304 | tf_op jit(solution)/shard_map/all_to_all | solution.py:112
  241.2 54.2 %reduce-scatter.3.cloned.1.call-start = ((), (), s32[]{:S(2)}) async-start(), calls=%async_computation.7 | async-start | bytes 1179648 | tf_op jit(solution)/shard_map/reduce_scatter | solution.py:129
  241.4 3.1 copy-start.5
  243.0 1.5 copy-start.10
  249.6 3.9 %copy-start.4 = (bf16[8,128,256]{1,2,0:T(8,128)(2,1)S(1)}, bf16[8,128,256]{1,2,0:T(8,128)(2,1)}, u32[]{:S(2)}) copy-start(bf16[8,128,256]{1,2,0:T(8,128)(2,1)} %copy-done.3) | copy-start | bytes 1572868
  253.5 83.7 %reduce-scatter.5.cloned.1.call-start = ((), (), s32[]{:S(2)}) async-start(), calls=%async_computation.8 | async-start | bytes 1179648 | tf_op jit(solution)/shard_map/reduce_scatter | solution.py:130
  253.6 1.6 copy-start.6
  253.6 2.8 copy-start.7
Sparse Core Ops, SparseCore 0:
  253.6 40.5 reduce-scatter.2
  297.0 40.1 reduce-scatter.4
